TPU v7x, 32 devices: a whole 2x2x4 slice. The times are simulated.
32 devices in a mesh: dp: 4 (over x, core), hidden: 8 (over z, y).
Axes of the slice: x: 2, y: 2, z: 4, core: 2. Of those that a mesh axis runs over, the one named last changes fastest.
Arguments:
- features: bfloat16 [32768, 16384], P('dp', 'hidden'), may hold values from -0.046875 to 0.046875
- codes: int32 [32768], P('dp'), may hold values from 1 to 8
- targets: float32 [16384, 32], P('hidden'), may hold values from -6 to 6
- guess: float32 [16384, 32], P('hidden'), may hold values from -4 to 4
Outputs:
- solution: float32 [16384, 32], P('hidden')
- residual: float32 [16384, 32], P('hidden')
All inputs are finite; a program needn't handle non-finite values.
Results may differ from a plain program's by a relative error of at most 0.011.
Values may be sent and summed in bfloat16 or wider, within the bound.
A program may use at most 128 MiB of HBM per device.

v0:
```python
import jax
import jax.numpy as jnp
from jax import lax
from jax.sharding import PartitionSpec as P

ITERS = 2


damping = 0.5
code_scale = 0.25


def apply_operator(features, weights, vectors):
    rounded = vectors.astype(jnp.bfloat16)
    partial_rows = jnp.dot(features, rounded, preferred_element_type=jnp.float32)
    summed = lax.psum(partial_rows, "hidden")
    scaled = (weights[:, None] * summed).astype(jnp.bfloat16)
    back = lax.dot_general(
        features, scaled, (((0,), (0,)), ((), ())), preferred_element_type=jnp.float32
    )
    total = lax.psum(back, "dp")
    return total + damping * vectors


def local_gram(left, right):
    return jnp.dot(left.T, right, precision=lax.Precision.HIGHEST)


def residual_gram(residual):
    return lax.psum(local_gram(residual, residual), "hidden")


def solve_small(matrix, rhs_block):
    factor = jnp.linalg.cholesky(0.5 * (matrix + matrix.T))
    middle = lax.linalg.triangular_solve(factor, rhs_block, left_side=True, lower=True)
    return lax.linalg.triangular_solve(factor, middle, left_side=True, lower=True, transpose_a=True)


def shards(features, codes, targets, guess):
    weights = codes.astype(jnp.float32) * code_scale
    solution = guess
    residual = targets - apply_operator(features, weights, guess)
    direction = residual
    norm_now = residual_gram(residual)
    for step in range(ITERS):
        applied = apply_operator(features, weights, direction)
        curv = lax.psum(local_gram(direction, applied), "hidden")
        step_mix = solve_small(curv, norm_now)
        solution = solution + jnp.dot(direction, step_mix, precision=lax.Precision.HIGHEST)
        residual = residual - jnp.dot(applied, step_mix, precision=lax.Precision.HIGHEST)
        if step + 1 < ITERS:
            fresh = residual_gram(residual)
            mixing = solve_small(norm_now, fresh)
            direction = residual + jnp.dot(direction, mixing, precision=lax.Precision.HIGHEST)
            norm_now = fresh
    return (solution, residual)


def solution(mesh):
    in_specs = (P("dp", "hidden"), P("dp"), P("hidden", None), P("hidden", None))
    out_specs = (P("hidden", None), P("hidden", None))
    return jax.shard_map(shards, mesh=mesh, in_specs=in_specs, out_specs=out_specs, check_vma=False)
```

profile of v0, /device:TPU:0, one launch (start us, length us, event | category | flops | bytes accessed | tf_op | source)
XLA Modules:
  0.0 586.1 jit_solution(132984846567422276)
XLA Ops:
  7.2 21.7 %fusion.11 = f32[8192,32]{0,1:T(8,128)} fusion(bf16[8192,2048]{1,0:T(8,128)(2,1)} %param.9, f32[2048,32]{0,1:T(8,128)} %param.12), kind=kOutput, calls=%fused_computation.27 | convolution fusion | flops 1073807360 | bytes 34865152 | tf_op jit(solution)/shard_map/dot_general | solution.py:15
  29.3 80.6 %all-reduce.8.cloned.1.call-done = f32[8192,32]{0,1:T(8,128)} async-done(((f32[8192,32]{0,1:T(8,128)}), f32[8192,32]{0,1:T(8,128)}) %all-reduce.8.cloned.1.call-update) | async-done | bytes 1048592 | tf_op jit(solution)/shard_map/psum | solution.py:16
  109.9 17.4 %convolution_bitcast_fusion.4 = f32[2048,32]{0,1:T(8,128)} fusion(bf16[8192,2048]{1,0:T(8,128)(2,1)} %param.9, f32[8192,32]{0,1:T(8,128)} %all-reduce.8.cloned.1.call-done, f32[8192]{0:T(1024)S(1)} %convert_multiply_fusion), kind=kOutput, calls=%fused_computation.4 | convolution fusion | flops 1074266112 | bytes 34897920 | tf_op jit(solution)/shard_map/dot_general | solution.py:18
  127.4 31.7 %all-reduce.10.cloned.1.call-done = f32[2048,32]{0,1:T(8,128)} async-done(((f32[2048,32]{0,1:T(8,128)}), f32[2048,32]{0,1:T(8,128)}) %all-reduce.10.cloned.1.call-update) | async-done | bytes 262160 | tf_op jit(solution)/shard_map/psum | solution.py:21
  160.1 15.6 %convolution_bitcast_fusion.1 = f32[8192,32]{0,1:T(8,128)} fusion(bf16[8192,2048]{1,0:T(8,128)(2,1)} %param.9, f32[2048,32]{0,1:T(8,128)S(1)} %add_subtract_fusion), kind=kOutput, calls=%fused_computation.1 | convolution fusion | flops 1073807360 | bytes 34865152 | tf_op jit(solution)/shard_map/dot_general | solution.py:15
  175.8 78.1 %all-reduce.12.cloned.1.call-done = f32[8192,32]{0,1:T(8,128)} async-done(((f32[8192,32]{0,1:T(8,128)}), f32[8192,32]{0,1:T(8,128)}) %all-reduce.12.cloned.1.call-update) | async-done | bytes 1048592 | tf_op jit(solution)/shard_map/psum | solution.py:16
  253.9 17.4 %convolution_bitcast_fusion.3 = f32[2048,32]{0,1:T(8,128)} fusion(bf16[8192,2048]{1,0:T(8,128)(2,1)} %param.9, f32[8192,32]{0,1:T(8,128)} %all-reduce.12.cloned.1.call-done, f32[8192]{0:T(1024)S(1)} %convert_multiply_fusion), kind=kOutput, calls=%fused_computation.3 | convolution fusion | flops 1074266112 | bytes 34897920 | tf_op jit(solution)/shard_map/dot_general | solution.py:18
  271.8 31.3 %all-reduce.14.cloned.1.call-done = f32[2048,32]{0,1:T(8,128)} async-done(((f32[2048,32]{0,1:T(8,128)}), f32[2048,32]{0,1:T(8,128)}) %all-reduce.14.cloned.1.call-update) | async-done | bytes 262160 | tf_op jit(solution)/shard_map/psum | solution.py:21
  303.1 1.3 fusion.3
  304.4 37.1 %all-reduce = (f32[32,32]{1,0:T(8,128)S(1)}, f32[32,32]{1,0:T(8,128)S(1)}) all-reduce(f32[32,32]{1,0:T(8,128)S(1)} %fusion.38, f32[32,32]{1,0:T(8,128)S(1)} %fusion.3), channel_id=1, replica_groups=mesh['dp'=4,'hidden'=8] {'hidden'}, use_global_device_ids=true, to_apply=%region_7.0 | all-reduce | flops 2048 | bytes 16384 | tf_op jit(solution)/shard_map/psum | solution.py:30
  341.8 2.9 cholesky.70
  346.0 2.4 custom-call.15
  348.6 2.9 cholesky.59
  352.8 2.4 custom-call.13
  355.7 1.4 convolution_subtract_fusion.1
  357.4 33.0 %psum.76 = f32[32,32]{1,0:T(8,128)S(1)} all-reduce(f32[32,32]{1,0:T(8,128)S(1)} %fusion.39), channel_id=1, replica_groups=mesh['dp'=4,'hidden'=8] {'hidden'}, use_global_device_ids=true, to_apply=%region_8.12 | all-reduce | flops 1024 | bytes 8192 | tf_op jit(solution)/shard_map/psum | solution.py:30
  391.2 15.6 %convolution_bitcast_fusion = f32[8192,32]{0,1:T(8,128)} fusion(bf16[8192,2048]{1,0:T(8,128)(2,1)} %param.9, f32[2048,32]{0,1:T(8,128)S(1)} %convolution_add_fusion.1), kind=kOutput, calls=%fused_computation | convolution fusion | flops 1073807360 | bytes 34865152 | tf_op jit(solution)/shard_map/dot_general | solution.py:15
  406.9 74.3 %all-reduce.16.cloned.1.call-done = f32[8192,32]{0,1:T(8,128)} async-done(((f32[8192,32]{0,1:T(8,128)}), f32[8192,32]{0,1:T(8,128)}) %all-reduce.16.cloned.1.call-update) | async-done | bytes 1048592 | tf_op jit(solution)/shard_map/psum | solution.py:16
  481.2 17.4 %convolution_bitcast_fusion.2 = f32[2048,32]{0,1:T(8,128)} fusion(bf16[8192,2048]{1,0:T(8,128)(2,1)} %param.9, f32[8192,32]{0,1:T(8,128)} %all-reduce.16.cloned.1.call-done, f32[8192]{0:T(1024)S(1)} %convert_multiply_fusion), kind=kOutput, calls=%fused_computation.2 | convolution fusion | flops 1074266112 | bytes 34897920 | tf_op jit(solution)/shard_map/dot_general | solution.py:18
  499.1 31.3 %all-reduce.18.cloned.1.call-done = f32[2048,32]{0,1:T(8,128)} async-done(((f32[2048,32]{0,1:T(8,128)}), f32[2048,32]{0,1:T(8,128)}) %all-reduce.18.cloned.1.call-update) | async-done | bytes 262160 | tf_op jit(solution)/shard_map/psum | solution.py:21
  531.7 37.1 %psum.79 = f32[32,32]{1,0:T(8,128)S(1)} all-reduce(f32[32,32]{1,0:T(8,128)S(1)} %fusion.4), channel_id=1, replica_groups=mesh['dp'=4,'hidden'=8] {'hidden'}, use_global_device_ids=true, to_apply=%region_11.15 | all-reduce | flops 1024 | bytes 8192 | tf_op jit(solution)/shard_map/psum | solution.py:47
  569.0 2.9 cholesky.81
  573.2 2.4 custom-call.17
  577.2 2.1 convolution_subtract_fusion
  (52 shorter events, 11.1 us)
Async XLA Ops:
  7.2 151.9 %copy-start = (f32[2048,32]{0,1:T(8,128)S(1)}, f32[2048,32]{0,1:T(8,128)}, u32[]{:S(2)}) copy-start(f32[2048,32]{0,1:T(8,128)} %param.12) | copy-start | bytes 786436
  7.2 22.1 %copy-start.2 = (s32[8192]{0:T(1024)S(1)}, s32[8192]{0:T(1024)}, u32[]{:S(2)}) copy-start(s32[8192]{0:T(1024)} %param.10) | copy-start | bytes 98308
  7.2 151.9 %copy-start.1 = (f32[2048,32]{0,1:T(8,128)S(1)}, f32[2048,32]{0,1:T(8,128)}, u32[]{:S(2)}) copy-start(f32[2048,32]{0,1:T(8,128)} %param.11) | copy-start | bytes 786436
  7.2 102.7 %all-reduce.8.cloned.1.call-start = ((), (), s32[]{:S(2)}) async-start(), calls=%async_computation | async-start | bytes 2097152 | tf_op jit(solution)/shard_map/psum | solution.py:16
  29.0 130.1 %all-reduce.10.cloned.1.call-start = ((), (), s32[]{:S(2)}) async-start(), calls=%async_computation.1 | async-start | bytes 524288 | tf_op jit(solution)/shard_map/psum | solution.py:21
  127.3 126.6 %all-reduce.12.cloned.1.call-start = ((), (), s32[]{:S(2)}) async-start(), calls=%async_computation.2 | async-start | bytes 2097152 | tf_op jit(solution)/shard_map/psum | solution.py:16
  175.7 127.4 %all-reduce.14.cloned.1.call-start = ((), (), s32[]{:S(2)}) async-start(), calls=%async_computation.3 | async-start | bytes 524288 | tf_op jit(solution)/shard_map/psum | solution.py:21
  271.4 209.8 %all-reduce.16.cloned.1.call-start = ((), (), s32[]{:S(2)}) async-start(), calls=%async_computation.4 | async-start | bytes 2097152 | tf_op jit(solution)/shard_map/psum | solution.py:16
  406.8 123.6 %all-reduce.18.cloned.1.call-start = ((), (), s32[]{:S(2)}) async-start(), calls=%async_computation.5 | async-start | bytes 524288 | tf_op jit(solution)/shard_map/psum | solution.py:21
Sparse Core Ops, SparseCore 0:
  29.1 80.7 all-reduce.7
  127.5 31.5 all-reduce.9
  175.8 78.0 all-reduce.11
  271.5 31.5 all-reduce.13
  407.0 74.2 all-reduce.15
  498.8 31.5 all-reduce.17
where the time goes:
time: 587 us; the launch traced here: 586 us
  waiting for transfers between devices  327 us (56%)
  matrix products  115 us (20%)
  blocking collectives  107 us (18%)
  other arithmetic  21.1 us (4%)
  between operations  14.3 us (2%)
    psum x3, waiting for transfers between devices, apply_operator(): summed = lax.psum(partial_rows, 'hidden')  233 us
    psum x3, waiting for transfers between devices, apply_operator(): total = lax.psum(back, 'dp')  94.3 us
    psum x2, blocking collectives, residual_gram(): return lax.psum(local_gram(residual, residual), 'hidden')  70.1 us
    dot_general x3, matrix products, apply_operator(): jnp.dot(features, rounded, preferred_element_type=jnp.float32)  53 us
    dot_general x3, matrix products, apply_operator(): lax.dot_general(features, scaled, (((0,), (0,)), ((), ())), preferred_ele...  52.3 us
    psum x1, blocking collectives, shards(): curv = lax.psum(local_gram(direction, applied), 'hidden')  37.1 us
  transfers between devices with their start and end apart: 6, of which 6 were waited for; matrix products, arithmetic and copies ran while one was open for 0% of the time, Pallas kernels for 0%

commit v1 on v0

v1 whole, which is shorter than its diff:
```python
import functools

import jax
import jax.numpy as jnp
from jax import lax
from jax.experimental import pallas as pl
from jax.experimental.pallas import tpu as pltpu
from jax.sharding import PartitionSpec as P

ITERS = 2
damping = 0.5
code_scale = 0.25

F32 = jnp.float32
BF16 = jnp.bfloat16
NT = (((1,), (1,)), ((), ()))
TN = (((0,), (0,)), ((), ()))


def exact(a, b, dims):
    return lax.dot_general(a, b, dims, precision=lax.Precision.HIGHEST, preferred_element_type=F32)


def solve_small(matrix, rhs):
    left = 0.5 * (matrix + matrix.T)
    right = rhs
    size = left.shape[0]
    row_at = lax.broadcasted_iota(jnp.int32, left.shape, 0)
    for k in range(size):
        here = row_at == k
        inv = 1.0 / left[k : k + 1, k : k + 1]
        lrow = left[k : k + 1, :] * inv
        rrow = right[k : k + 1, :] * inv
        col = left[:, k : k + 1]
        left = jnp.where(here, lrow, left - col * lrow)
        right = jnp.where(here, rrow, right - col * rrow)
    return right


def kernel(nh, nd, f_hbm, codes_ref, t_ref, g_ref, sol_ref, res_ref,
           fv, rs_send, rs_recv, own, rows0, gr_send, gr_recv, ag, pg_send, pg_recv,
           acc, dr_recv, dg_send, dg_recv, dq, d_ref,
           f_sem, rs_ss, rs_rs, gr_ss, gr_rs, ag_ss, ag_rs, pg_ss, pg_rs,
           dr_ss, dr_rs, dg_ss, dg_rs, dq_ss, dq_rs):
    me = lax.axis_index("hidden")
    md = lax.axis_index("dp")
    tokens, width = fv.shape
    seg = tokens // nh
    part = width // nd

    def at_step(i):
        return ((i + nh // 2 - 1) % (nh - 1) + 1) * (1 - i // (nh - 1))

    def rows_of(index):
        return pl.ds(pl.multiple_of(index * seg, seg), seg)

    def f_copy(i):
        t = rows_of((me + at_step(i)) % nh)
        return pltpu.make_async_copy(f_hbm.at[t], fv.at[t], f_sem.at[i])

    def to_hidden(src, dst, ss, rs, d):
        return pltpu.make_async_remote_copy(
            src_ref=src, dst_ref=dst, send_sem=ss.at[d], recv_sem=rs.at[d],
            device_id={"hidden": (me + d) % nh}, device_id_type=pl.DeviceIdType.MESH)

    def to_dp(src, dst, ss, rs, e):
        return pltpu.make_async_remote_copy(
            src_ref=src, dst_ref=dst, send_sem=ss.at[e], recv_sem=rs.at[e],
            device_id={"dp": (md + e) % nd}, device_id_type=pl.DeviceIdType.MESH)

    rs_copy = lambda d: to_hidden(rs_send.at[d], rs_recv.at[d], rs_ss, rs_rs, d)
    gr_copy = lambda d: to_hidden(gr_send, gr_recv.at[d], gr_ss, gr_rs, d)
    ag_copy = lambda d: to_hidden(ag.at[0], ag.at[d], ag_ss, ag_rs, d)
    pg_copy = lambda d: to_hidden(pg_send, pg_recv.at[d], pg_ss, pg_rs, d)
    dr_copy = lambda e: to_dp(acc.at[(md + e) % nd], dr_recv.at[e], dr_ss, dr_rs, e)
    dg_copy = lambda k, e: to_dp(dg_send, dg_recv.at[k - 1, e], dg_ss.at[k - 1], dg_rs.at[k - 1], e)
    dq_send = lambda e: to_dp(dq.at[md], dq.at[md], dq_ss, dq_rs, e)
    dq_got = lambda e: to_dp(dq.at[md], dq.at[(md + nd - e) % nd], dq_ss, dq_rs, e)

    def each(start, stop, fn):
        def body(i, _):
            fn(i)
            return 0
        lax.fori_loop(start, stop, body, 0)

    each(0, nh, lambda i: f_copy(i).start())

    barrier = pltpu.get_barrier_semaphore()
    each(1, nh, lambda d: pl.semaphore_signal(
        barrier, inc=1, device_id={"hidden": (me + d) % nh}, device_id_type=pl.DeviceIdType.MESH))
    each(1, nd, lambda e: pl.semaphore_signal(
        barrier, inc=1, device_id={"dp": (md + e) % nd}, device_id_type=pl.DeviceIdType.MESH))
    pl.semaphore_wait(barrier, nh - 1 + nd - 1)

    weights = codes_ref[me].astype(F32) * code_scale

    norms = None
    for k in range(ITERS + 1):
        source = g_ref if k == 0 else res_ref
        vec = source[...].astype(BF16)
        if k > 0:
            gr_send[...] = exact(source[...], source[...], NT)
            each(1, nh, lambda d: gr_copy(d).start())

        def forward(i):
            d = at_step(i)
            if k == 0:
                f_copy(i).wait()
            r = lax.dot_general(vec, fv[rows_of((me + d) % nh), :], NT, preferred_element_type=F32)
            own[...] = r
            rs_send[d] = r.astype(BF16)

            @pl.when(i < nh - 1)
            def _():
                rs_copy(d).start()

        each(0, nh, forward)

        if k > 0:
            each(1, nh, lambda d: gr_copy(d).wait())
            fresh = gr_send[...]
            for d in range(1, nh):
                fresh = fresh + gr_recv[d]
            if k > 1:
                mix = solve_small(norms, fresh)
                d_ref[...] = res_ref[...] + exact(mix, d_ref[...], TN)
            norms = fresh

        each(1, nh, lambda i: rs_copy(i).wait())
        rows = own[...]
        for d in range(1, nh):
            rows = rows + rs_recv[d].astype(F32)
        if k > 1:
            rows = rows + exact(mix, rows0[...], TN)
        if 0 < k < ITERS:
            rows0[...] = rows
        scaled = (rows * weights).astype(BF16)
        ag[0] = scaled
        each(0, nh - 1, lambda i: ag_copy(at_step(i)).start())
        if k > 0:
            local = gr_send[...] if k == 1 else exact(d_ref[...], d_ref[...], NT)
            pg_send[...] = exact(rows, scaled.astype(F32), NT) + (damping / nd) * local
            each(1, nh, lambda d: pg_copy(d).start())

        def add_back(d, first):
            seg_rows = rows_of((me + nh - d) % nh)
            piece = ag[d]
            for c in range(nd):
                got = jnp.dot(piece, fv[seg_rows, c * part : (c + 1) * part], preferred_element_type=F32)
                acc[c] = got if first else acc[c] + got

        add_back(0, True)

        def backward(i):
            d = at_step(i)
            ag_copy(d).wait()
            add_back(d, False)

        each(0, nh - 1, backward)
        each(1, nd, lambda e: dr_copy(e).start())
        if k > 0:
            each(1, nh, lambda d: pg_copy(d).wait())
            dg = pg_send[...]
            for d in range(1, nh):
                dg = dg + pg_recv[d]
            dg_send[...] = dg
            each(1, nd, lambda e: dg_copy(k, e).start())
        each(1, nd, lambda e: dr_copy(e).wait())
        total = acc[md]
        for e in range(1, nd):
            total = total + dr_recv[e]
        dq[md] = total
        each(1, nd, lambda e: dq_send(e).start())
        if k > 0:
            each(1, nd, lambda e: dg_copy(k, e).wait())
            curv = dg_send[...]
            for e in range(1, nd):
                curv = curv + dg_recv[k - 1, e]
            step_mix = solve_small(curv, norms)
        each(1, nd, lambda e: dq_got(e).wait())
        applied = jnp.concatenate([dq[c] for c in range(nd)], axis=1)
        if k == 0:
            residual = t_ref[...] - (applied + damping * g_ref[...])
            res_ref[...] = residual
            d_ref[...] = residual
        else:
            applied = applied + damping * d_ref[...]
            before = g_ref[...] if k == 1 else sol_ref[...]
            sol_ref[...] = before + exact(step_mix, d_ref[...], TN)
            res_ref[...] = res_ref[...] - exact(step_mix, applied, TN)


def shards(nh, nd, features, codes, targets, guess):
    tokens, width = features.shape
    rhs = guess.shape[1]
    seg = tokens // nh
    part = width // nd
    vmem = pl.BlockSpec(memory_space=pltpu.VMEM)
    flat = jax.ShapeDtypeStruct((rhs, width), F32)
    dma = pltpu.SemaphoreType.DMA
    sol, res = pl.pallas_call(
        functools.partial(kernel, nh, nd),
        out_shape=(flat, flat),
        in_specs=[pl.BlockSpec(memory_space=pl.ANY), vmem, vmem, vmem],
        out_specs=(vmem, vmem),
        scratch_shapes=[
            pltpu.VMEM((tokens, width), BF16),
            pltpu.VMEM((nh, rhs, seg), BF16),
            pltpu.VMEM((nh, rhs, seg), BF16),
            pltpu.VMEM((rhs, seg), F32),
            pltpu.VMEM((rhs, seg), F32),
            pltpu.VMEM((rhs, rhs), F32),
            pltpu.VMEM((nh, rhs, rhs), F32),
            pltpu.VMEM((nh, rhs, seg), BF16),
            pltpu.VMEM((rhs, rhs), F32),
            pltpu.VMEM((nh, rhs, rhs), F32),
            pltpu.VMEM((nd, rhs, part), F32),
            pltpu.VMEM((nd, rhs, part), F32),
            pltpu.VMEM((rhs, rhs), F32),
            pltpu.VMEM((ITERS, nd, rhs, rhs), F32),
            pltpu.VMEM((nd, rhs, part), F32),
            pltpu.VMEM((rhs, width), F32),
            dma((nh,)),
            dma((nh,)), dma((nh,)), dma((nh,)), dma((nh,)),
            dma((nh,)), dma((nh,)), dma((nh,)), dma((nh,)),
            dma((nd,)), dma((nd,)), dma((ITERS, nd)), dma((ITERS, nd)), dma((nd,)), dma((nd,)),
        ],
        compiler_params=pltpu.CompilerParams(
            collective_id=0, has_side_effects=True, vmem_limit_bytes=56 * 1024 * 1024),
        cost_estimate=pl.CostEstimate(
            flops=12 * tokens * width * rhs, bytes_accessed=2 * tokens * width, transcendentals=0),
    )(features, codes.reshape(nh, 1, seg), targets.T, guess.T)
    return sol.T, res.T


def solution(mesh):
    nh, nd = mesh.shape["hidden"], mesh.shape["dp"]
    in_specs = (P("dp", "hidden"), P("dp"), P("hidden", None), P("hidden", None))
    out_specs = (P("hidden", None), P("hidden", None))
    return jax.shard_map(functools.partial(shards, nh, nd), mesh=mesh, in_specs=in_specs,
                         out_specs=out_specs, check_vma=False)
```

time: 587 us -> 133 us (0.23)
  waiting for transfers between devices: 327 us -> 0 us
  Pallas kernels: 0 us -> 128 us
  matrix products: 115 us -> 0 us
  blocking collectives: 107 us -> 0 us
  other arithmetic: 21.1 us -> 0 us
  between operations: 14.3 us -> 0.64 us
    psum x6 -> x0, waiting for transfers between devices: 327 us -> none  [the longest x3 233 us: apply_operator(): summed = lax.psum(partial_rows, 'hidden')]
    pallas_call x0 -> x1, Pallas kernels: none -> 128 us  [shards(): pl.pallas_call(functools.partial(kernel, nh, nd), out_shape=(flat, flat),...]
    dot_general x15 -> x0, matrix products: 114 us -> none  [the longest x3 53 us: apply_operator(): jnp.dot(features, rounded, preferred_element_type=jnp.float32)]
    psum x3 -> x0, blocking collectives: 107 us -> none  [the longest x2 70.1 us: residual_gram(): return lax.psum(local_gram(residual, residual), 'hidden')]
    another operation x15 -> x0, other arithmetic: 20.1 us -> none  [the longest x9 10.8 us: solve_small(): factor = jnp.linalg.cholesky(0.5 * (matrix + matrix.T))]
  transfers between devices with their start and end apart: 6 -> 0, of which waited for: 6 -> 0; matrix products, arithmetic and copies ran while one was open for 0% -> 0% of each run, Pallas kernels for 0% -> 0%
where the time goes in v1:
time: 133 us; the launch traced here: 132 us
  Pallas kernels  128 us (96%)
  local copies, waits for them, and re-layouts  3.34 us (3%)
    pallas_call x1, Pallas kernels, shards(): pl.pallas_call(functools.partial(kernel, nh, nd), out_shape=(flat, flat),...  128 us
    unnamed x2, local copies, waits for them, and re-layouts  3.34 us

profile of v1, /device:TPU:0, one launch (start us, length us, event | category | flops | bytes accessed | tf_op | source)
XLA Modules:
  0.0 132.1 jit_solution(6149475164238609960)
XLA Ops:
  0.6 128.1 %shard_map.59 = (f32[32,2048]{1,0:T(8,128)}, f32[32,2048]{1,0:T(8,128)}) custom-call(bf16[8192,2048]{1,0:T(8,128)(2,1)} %f_hbm.1, s32[8,1,1024]{2,1,0:T(1,128)} %bitcast.9, f32[32,2048]{1,0:T(8,128)} %bitcast.5, f32[32,2048]{1,0:T(8,128)} %bitcast.6), custom_call_target="tpu_custom_call" | custom-call | flops 6442450944 | bytes 33554432 | tf_op jit(solution)/shard_map/pallas_call | solution.py:201
  128.7 1.7 %copy.8 = f32[2048,32]{0,1:T(8,128)} copy(f32[2048,32]{0,1:T(8,128)} %bitcast.8) | data formatting | bytes 524288
  130.4 1.7 %copy.9 = f32[2048,32]{0,1:T(8,128)} copy(f32[2048,32]{0,1:T(8,128)} %bitcast.7) | data formatting | bytes 524288

commit v2 on v1

--- a/solution.py
+++ b/solution.py
@@ -39,7 +39,7 @@
 
 def kernel(nh, nd, f_hbm, codes_ref, t_ref, g_ref, sol_ref, res_ref,
            fv, rs_send, rs_recv, own, rows0, gr_send, gr_recv, ag, pg_send, pg_recv,
-           acc, dr_recv, dg_send, dg_recv, dq, d_ref,
+           acc, dr_send, dr_recv, dg_send, dg_recv, dq, d_ref,
            f_sem, rs_ss, rs_rs, gr_ss, gr_rs, ag_ss, ag_rs, pg_ss, pg_rs,
            dr_ss, dr_rs, dg_ss, dg_rs, dq_ss, dq_rs):
     me = lax.axis_index("hidden")
@@ -70,9 +70,20 @@
 
     rs_copy = lambda d: to_hidden(rs_send.at[d], rs_recv.at[d], rs_ss, rs_rs, d)
     gr_copy = lambda d: to_hidden(gr_send, gr_recv.at[d], gr_ss, gr_rs, d)
-    ag_copy = lambda d: to_hidden(ag.at[0], ag.at[d], ag_ss, ag_rs, d)
+
+    nz = 4 if nh % 4 == 0 else 1
+    ny = nh // nz
+
+    def ag_copy(s):
+        dz, dy = s // ny, s % ny
+        handed = (dy + ny - 1) // ny
+        to = (me // ny + dz * (1 - handed)) % nz * ny + (me % ny + dy) % ny
+        return pltpu.make_async_remote_copy(
+            src_ref=ag.at[dz * ny * handed], dst_ref=ag.at[s], send_sem=ag_ss.at[s], recv_sem=ag_rs.at[s],
+            device_id={"hidden": to}, device_id_type=pl.DeviceIdType.MESH)
+
     pg_copy = lambda d: to_hidden(pg_send, pg_recv.at[d], pg_ss, pg_rs, d)
-    dr_copy = lambda e: to_dp(acc.at[(md + e) % nd], dr_recv.at[e], dr_ss, dr_rs, e)
+    dr_copy = lambda e: to_dp(dr_send.at[e], dr_recv.at[e], dr_ss, dr_rs, e)
     dg_copy = lambda k, e: to_dp(dg_send, dg_recv.at[k - 1, e], dg_ss.at[k - 1], dg_rs.at[k - 1], e)
     dq_send = lambda e: to_dp(dq.at[md], dq.at[md], dq_ss, dq_rs, e)
     dq_got = lambda e: to_dp(dq.at[md], dq.at[(md + nd - e) % nd], dq_ss, dq_rs, e)
@@ -136,28 +147,56 @@
             rows0[...] = rows
         scaled = (rows * weights).astype(BF16)
         ag[0] = scaled
-        each(0, nh - 1, lambda i: ag_copy(at_step(i)).start())
+        each(0, nz - 1, lambda i: ag_copy(((i + nz // 2 - 1) % (nz - 1) + 1) * ny).start())
+        each(1, ny, lambda s: ag_copy(s).start())
         if k > 0:
             local = gr_send[...] if k == 1 else exact(d_ref[...], d_ref[...], NT)
             pg_send[...] = exact(rows, scaled.astype(F32), NT) + (damping / nd) * local
             each(1, nh, lambda d: pg_copy(d).start())
 
-        def add_back(d, first):
-            seg_rows = rows_of((me + nh - d) % nh)
-            piece = ag[d]
+        def came_from(s):
+            return (me // ny + nz - s // ny) % nz * ny + (me % ny + ny - s % ny) % ny
+
+        def add_back(s, first):
+            seg_rows = rows_of(came_from(s))
+            piece = ag[s]
             for c in range(nd):
                 got = jnp.dot(piece, fv[seg_rows, c * part : (c + 1) * part], preferred_element_type=F32)
                 acc[c] = got if first else acc[c] + got
 
         add_back(0, True)
 
-        def backward(i):
-            d = at_step(i)
-            ag_copy(d).wait()
-            add_back(d, False)
-
-        each(0, nh - 1, backward)
-        each(1, nd, lambda e: dr_copy(e).start())
+        def passing(i):
+            s = ((i + nz // 2 - 1) % (nz - 1) + 1) * ny
+            ag_copy(s).wait()
+            each(1, ny, lambda dy: ag_copy(s + dy).start())
+            add_back(s, False)
+
+        def ending(i):
+            s = i // (ny - 1) * ny + i % (ny - 1) + 1
+            ag_copy(s).wait()
+            add_back(s, False)
+
+        each(0, nz - 1, passing)
+        each(0, nz * (ny - 1) - 2, ending)
+        last = [nh - 3 if ny == 2 else nh - 2, nh - 1]
+        for s in last:
+            ag_copy(s).wait()
+
+        def final(e):
+            c = (md + e) % nd
+            columns = pl.ds(pl.multiple_of(c * part, part), part)
+            got = acc[c]
+            for s in last:
+                got = got + jnp.dot(ag[s], fv[rows_of(came_from(s)), columns], preferred_element_type=F32)
+            return got
+
+        def finish(i):
+            dr_send[i] = final(i).astype(BF16)
+            dr_copy(i).start()
+
+        each(1, nd, finish)
+        total = final(0)
         if k > 0:
             each(1, nh, lambda d: pg_copy(d).wait())
             dg = pg_send[...]
@@ -166,9 +205,8 @@
             dg_send[...] = dg
             each(1, nd, lambda e: dg_copy(k, e).start())
         each(1, nd, lambda e: dr_copy(e).wait())
-        total = acc[md]
         for e in range(1, nd):
-            total = total + dr_recv[e]
+            total = total + dr_recv[e].astype(F32)
         dq[md] = total
         each(1, nd, lambda e: dq_send(e).start())
         if k > 0:
@@ -215,7 +253,8 @@
             pltpu.VMEM((rhs, rhs), F32),
             pltpu.VMEM((nh, rhs, rhs), F32),
             pltpu.VMEM((nd, rhs, part), F32),
-            pltpu.VMEM((nd, rhs, part), F32),
+            pltpu.VMEM((nd, rhs, part), BF16),
+            pltpu.VMEM((nd, rhs, part), BF16),
             pltpu.VMEM((rhs, rhs), F32),
             pltpu.VMEM((ITERS, nd, rhs, rhs), F32),
             pltpu.VMEM((nd, rhs, part), F32),

time: 133 us -> 126 us (0.947)
  Pallas kernels: 128 us -> 121 us
    pallas_call x1, Pallas kernels: 128 us -> 121 us  [shards(): pl.pallas_call(functools.partial(kernel, nh, nd), out_shape=(flat, flat),...]
where the time goes in v2:
time: 126 us; the launch traced here: 124 us
  Pallas kernels  121 us (96%)
  local copies, waits for them, and re-layouts  3.34 us (3%)
    pallas_call x1, Pallas kernels, shards(): pl.pallas_call(functools.partial(kernel, nh, nd), out_shape=(flat, flat),...  121 us
    unnamed x2, local copies, waits for them, and re-layouts  3.34 us

profile of v2, /device:TPU:0, one launch (start us, length us, event | category | flops | bytes accessed | tf_op | source)
XLA Modules:
  0.0 124.5 jit_solution(972635592232402508)
XLA Ops:
  0.6 120.5 %shard_map.59 = (f32[32,2048]{1,0:T(8,128)}, f32[32,2048]{1,0:T(8,128)}) custom-call(bf16[8192,2048]{1,0:T(8,128)(2,1)} %f_hbm.1, s32[8,1,1024]{2,1,0:T(1,128)} %bitcast.9, f32[32,2048]{1,0:T(8,128)} %bitcast.5, f32[32,2048]{1,0:T(8,128)} %bitcast.6), custom_call_target="tpu_custom_call" | custom-call | flops 6442450944 | bytes 33554432 | tf_op jit(solution)/shard_map/pallas_call | solution.py:239
  121.2 1.7 %copy.8 = f32[2048,32]{0,1:T(8,128)} copy(f32[2048,32]{0,1:T(8,128)} %bitcast.8) | data formatting | bytes 524288
  122.8 1.7 %copy.9 = f32[2048,32]{0,1:T(8,128)} copy(f32[2048,32]{0,1:T(8,128)} %bitcast.7) | data formatting | bytes 524288

commit v3 on v2

--- a/solution.py
+++ b/solution.py
@@ -179,7 +179,7 @@
 
         each(0, nz - 1, passing)
         each(0, nz * (ny - 1) - 2, ending)
-        last = [nh - 3 if ny == 2 else nh - 2, nh - 1]
+        last = [nh - 3, nh - 1] if ny == 2 else [nh - 2, nh - 1]
         for s in last:
             ag_copy(s).wait()
 
@@ -207,7 +207,7 @@
         each(1, nd, lambda e: dr_copy(e).wait())
         for e in range(1, nd):
             total = total + dr_recv[e].astype(F32)
-        dq[md] = total
+        dq[md] = total.astype(BF16)
         each(1, nd, lambda e: dq_send(e).start())
         if k > 0:
             each(1, nd, lambda e: dg_copy(k, e).wait())
@@ -216,7 +216,7 @@
                 curv = curv + dg_recv[k - 1, e]
             step_mix = solve_small(curv, norms)
         each(1, nd, lambda e: dq_got(e).wait())
-        applied = jnp.concatenate([dq[c] for c in range(nd)], axis=1)
+        applied = jnp.concatenate([dq[c].astype(F32) for c in range(nd)], axis=1)
         if k == 0:
             residual = t_ref[...] - (applied + damping * g_ref[...])
             res_ref[...] = residual
@@ -257,7 +257,7 @@
             pltpu.VMEM((nd, rhs, part), BF16),
             pltpu.VMEM((rhs, rhs), F32),
             pltpu.VMEM((ITERS, nd, rhs, rhs), F32),
-            pltpu.VMEM((nd, rhs, part), F32),
+            pltpu.VMEM((nd, rhs, part), BF16),
             pltpu.VMEM((rhs, width), F32),
             dma((nh,)),
             dma((nh,)), dma((nh,)), dma((nh,)), dma((nh,)),

time: 126 us -> 123 us (0.976); the launches traced: 124 us -> 123 us
  Pallas kernels: 121 us -> 119 us
    pallas_call x1, Pallas kernels: 121 us -> 119 us  [shards(): pl.pallas_call(functools.partial(kernel, nh, nd), out_shape=(flat, flat),...]
where the time goes in v3:
time: 123 us
  Pallas kernels  119 us (97%)
  local copies, waits for them, and re-layouts  3.34 us (3%)
    pallas_call x1, Pallas kernels, shards(): pl.pallas_call(functools.partial(kernel, nh, nd), out_shape=(flat, flat),...  119 us
    unnamed x2, local copies, waits for them, and re-layouts  3.34 us

profile of v3, /device:TPU:0, one launch (start us, length us, event | category | flops | bytes accessed | tf_op | source)
XLA Modules:
  0.0 123.2 jit_solution(7292194449289665733)
XLA Ops:
  0.6 119.2 %shard_map.59 = (f32[32,2048]{1,0:T(8,128)}, f32[32,2048]{1,0:T(8,128)}) custom-call(bf16[8192,2048]{1,0:T(8,128)(2,1)} %f_hbm.1, s32[8,1,1024]{2,1,0:T(1,128)} %bitcast.9, f32[32,2048]{1,0:T(8,128)} %bitcast.5, f32[32,2048]{1,0:T(8,128)} %bitcast.6), custom_call_target="tpu_custom_call" | custom-call | flops 6442450944 | bytes 33554432 | tf_op jit(solution)/shard_map/pallas_call | solution.py:239
  119.8 1.7 %copy.8 = f32[2048,32]{0,1:T(8,128)} copy(f32[2048,32]{0,1:T(8,128)} %bitcast.8) | data formatting | bytes 524288
  121.5 1.7 %copy.9 = f32[2048,32]{0,1:T(8,128)} copy(f32[2048,32]{0,1:T(8,128)} %bitcast.7) | data formatting | bytes 524288
